TPU v7x, 32 devices: a whole 2x2x4 slice. The times are simulated.
32 devices in a mesh: fsdp: 4 (over z), dp: 8 (over y, x, core).
Axes of the slice: x: 2, y: 2, z: 4, core: 2. Of those that a mesh axis runs over, the one named last changes fastest.
Arguments:
- tokens: bfloat16 [8, 1536, 896], P('dp', 'fsdp'), may hold values from -6 to 6
- cotangent: bfloat16 [8, 1536, 896], P('dp', 'fsdp'), may hold values from -6 to 6
- counts: int32 [8, 4], P('dp'), may hold values from 192 to 384, as said below
- lengths: int32 [8, 3], P('dp'), may hold values from 1 to 1056, as said below
- attn_gain: bfloat16 [896], P('dp'), may hold values from 0.5 to 1.5
- w_query: bfloat16 [896, 896], P('fsdp', 'dp'), may hold values from -0.1875 to 0.1875
- b_query: bfloat16 [896], P('dp'), may hold values from -3 to 3
- w_key: bfloat16 [896, 128], P('fsdp', 'dp'), may hold values from -0.1875 to 0.1875
- w_value: bfloat16 [896, 128], P('fsdp', 'dp'), may hold values from -0.1875 to 0.1875
- b_value: bfloat16 [128], P('dp'), may hold values from -3 to 3
- w_out: bfloat16 [896, 896], P('fsdp', 'dp'), may hold values from -0.5 to 0.5
- mlp_gain: bfloat16 [896], P('dp'), may hold values from 0.5 to 1.5
- w_gate: bfloat16 [896, 4864], P('fsdp', 'dp'), may hold values from -0.1875 to 0.1875
- w_up: bfloat16 [896, 4864], P('fsdp', 'dp'), may hold values from -0.1875 to 0.1875
- w_down: bfloat16 [4864, 896], P('fsdp', 'dp'), may hold values from -0.15625 to 0.15625
Outputs:
- mixed: bfloat16 [8, 1536, 896], P('dp', 'fsdp')
- d_tokens: bfloat16 [8, 1536, 896], P('dp', 'fsdp')
- grad_attn_gain: float32 [896], P('dp')
- grad_w_query: float32 [896, 896], P('fsdp', 'dp')
- grad_b_query: float32 [896], P('dp')
- grad_w_key: float32 [896, 128], P('fsdp', 'dp')
- grad_w_value: float32 [896, 128], P('fsdp', 'dp')
- grad_b_value: float32 [128], P('dp')
- grad_w_out: float32 [896, 896], P('fsdp', 'dp')
- grad_mlp_gain: float32 [896], P('dp')
- grad_w_gate: float32 [896, 4864], P('fsdp', 'dp')
- grad_w_up: float32 [896, 4864], P('fsdp', 'dp')
- grad_w_down: float32 [4864, 896], P('fsdp', 'dp')
Inputs may be any that keep to these rules, and one draw needn't show every extreme that they name: In each group the counts sum to 1152, and one count of each group equals 384. In each group the lengths sum to the group's used slots; the sequences fill the used slots of the devices in order; one sequence of each group has exactly the largest length and has tokens on the first and on the last device of fsdp.
All inputs are finite; a program needn't handle non-finite values.
Results may differ from a plain program's by a relative error of at most 0.02.
Values may be sent and summed in bfloat16 or wider, within the bound.
No kernel may reach another device: no remote copies, remote signals or barrier semaphores. Data moves between devices by JAX's collectives and lax.ppermute only.
A program may use at most 192 MiB of HBM per device.

v0:
```python
import jax
import jax.numpy as jnp
from jax import lax
from jax.sharding import PartitionSpec as P

QUERY_HEADS = 14
KEY_VALUE_HEADS = 2
HEAD_SIZE = 64


EPS = 1e-06
THETA = 1000000.0
NEGATIVE_FILL = -1e30


def shortened(array):
    return jax.tree.map(lambda a: a.astype(jnp.bfloat16) if a.dtype == jnp.float32 else a, array)


def token_meta(count_row, length_row, slot, per_device):
    device = slot // per_device
    inner = slot % per_device
    owners = jnp.arange(count_row.shape[0], dtype=jnp.int32)
    pick = (device[:, None] == owners[None, :]).astype(jnp.int32)
    before = jnp.cumsum(count_row) - count_row
    count_here = jnp.sum(pick * count_row[None, :], 1)
    offset = jnp.sum(pick * before[None, :], 1)
    valid_mask = inner < count_here
    block_index = offset + inner
    ends = jnp.cumsum(length_row)
    sequence_ids = jnp.sum((block_index[:, None] >= ends[None, :]).astype(jnp.int32), 1)
    starts = ends - length_row
    numbers = jnp.arange(length_row.shape[0], dtype=jnp.int32)
    start_of = jnp.sum(
        (sequence_ids[:, None] == numbers[None, :]).astype(jnp.int32) * starts[None, :], 1
    )
    position = jnp.where(valid_mask, block_index - start_of, 0)
    sequence_ids = jnp.where(valid_mask, sequence_ids, -1)
    return (valid_mask, block_index, sequence_ids, position)


def allowed_pairs(query_meta, key_meta):
    q_valid, q_index, q_seq, q_slot = query_meta
    k_valid, k_index, k_seq, k_slot = key_meta
    same = (q_seq[:, None] == k_seq[None, :]) & q_valid[:, None] & k_valid[None, :]
    same = same & (k_index[None, :] <= q_index[:, None])
    return same | (q_slot[:, None] == k_slot[None, :])


def rope_tables(position, half):
    steps = jnp.arange(half, dtype=jnp.float32) * (1.0 / half)
    freq = THETA ** (-steps)
    angle = position[:, None] * freq[None, :]
    cosine_table = jnp.cos(angle)
    sine_table = jnp.sin(angle)
    return (
        jnp.concatenate([cosine_table, cosine_table], 1),
        jnp.concatenate([sine_table, sine_table], 1),
    )


def table_shape(tensor):
    return (tensor.shape[0],) + (1,) * (tensor.ndim - 2) + (tensor.shape[-1],)


def rotary_apply(tensor, cosine_table, sine_table):
    half = tensor.shape[-1] // 2
    turned = jnp.concatenate([-tensor[..., half:], tensor[..., :half]], -1)
    shape = table_shape(tensor)
    return tensor * cosine_table.reshape(shape) + turned * sine_table.reshape(shape)


def rotary_reverse(tensor, cosine_table, sine_table):
    half = tensor.shape[-1] // 2
    shape = table_shape(tensor)
    moved = tensor * sine_table.reshape(shape)
    turned = jnp.concatenate([moved[..., half:], -moved[..., :half]], -1)
    return tensor * cosine_table.reshape(shape) + turned


def alternate(parts, lanes):
    token_count = parts[0].shape[0]
    return jnp.concatenate([p.reshape(token_count, lanes, -1) for p in parts], 2).reshape(
        token_count, -1
    )


def split_lanes(whole, widths, lanes):
    token_count = whole.shape[0]
    cube = whole.reshape(token_count, lanes, -1)
    pieces = []
    offset = 0
    for width in widths:
        pieces.append(cube[:, :, offset : offset + width].reshape(token_count, -1))
        offset = offset + width
    return pieces


def spread_columns(left, slab):
    return jnp.dot(
        left, lax.all_gather(slab, "dp", axis=1, tiled=True), preferred_element_type=jnp.float32
    )


def fold_columns(grad, slab):
    return lax.dot_general(
        grad,
        lax.all_gather(slab, "dp", axis=1, tiled=True),
        (((1,), (1,)), ((), ())),
        preferred_element_type=jnp.float32,
    )


def column_terms(left, grad):
    return lax.psum_scatter(
        lax.dot_general(
            grad, left, (((0,), (0,)), ((), ())), preferred_element_type=jnp.float32
        ).astype(jnp.bfloat16),
        "dp",
        scatter_dimension=0,
        tiled=True,
    ).astype(jnp.float32)


def weight_grads(pairs):
    terms = tuple((column_terms(left, grad) for left, grad in pairs))
    summed = jax.tree.map(
        lambda part: part.astype(jnp.float32),
        lax.psum_scatter(shortened(terms), "fsdp", scatter_dimension=1, tiled=True),
    )
    return tuple((jnp.transpose(s) for s in summed))


def body(
    tokens,
    cotangent,
    counts,
    lengths,
    attn_gain,
    w_query,
    b_query,
    w_key,
    w_value,
    b_value,
    w_out,
    mlp_gain,
    w_gate,
    w_up,
    w_down,
):
    lanes = lax.axis_size("dp")
    fsdp_place = lax.axis_index("fsdp")
    token_rows = tokens.shape[1]
    grouped_rows = token_rows * lax.axis_size("fsdp")
    head_groups = QUERY_HEADS // KEY_VALUE_HEADS
    scale = float(HEAD_SIZE) ** (-0.5)
    inputs = tokens[0].astype(jnp.float32)
    group_slots = jnp.arange(grouped_rows, dtype=jnp.int32)
    k_valid, k_index, k_seq, k_pos = token_meta(counts[0], lengths[0], group_slots, token_rows)
    own_start = fsdp_place * token_rows
    q_valid = lax.dynamic_slice_in_dim(k_valid, own_start, token_rows)
    q_index = lax.dynamic_slice_in_dim(k_index, own_start, token_rows)
    q_seq = lax.dynamic_slice_in_dim(k_seq, own_start, token_rows)
    q_pos = lax.dynamic_slice_in_dim(k_pos, own_start, token_rows)
    q_slot = lax.dynamic_slice_in_dim(group_slots, own_start, token_rows)
    query_meta = (q_valid, q_index, q_seq, q_slot)
    valid_col = q_valid.astype(jnp.float32)[:, None]
    vectors = (
        lax.all_gather(attn_gain, "dp", axis=0, tiled=True),
        lax.all_gather(b_query, "dp", axis=0, tiled=True),
        lax.all_gather(b_value, "dp", axis=0, tiled=True),
        lax.all_gather(mlp_gain, "dp", axis=0, tiled=True),
    )
    gain_one, query_bias_vector, bias_value, gain_two = [v.astype(jnp.float32) for v in vectors]
    matrices = (w_query, w_key, w_value, w_out, w_gate, w_up, w_down)
    slabs = (
        lax.all_gather(matrices[0], "fsdp", axis=0, tiled=True),
        lax.all_gather(matrices[1], "fsdp", axis=0, tiled=True),
        lax.all_gather(matrices[2], "fsdp", axis=0, tiled=True),
        lax.all_gather(matrices[3], "fsdp", axis=0, tiled=True),
        lax.all_gather(matrices[4], "fsdp", axis=0, tiled=True),
        lax.all_gather(matrices[5], "fsdp", axis=0, tiled=True),
        lax.all_gather(matrices[6], "fsdp", axis=0, tiled=True),
    )
    joint_widths = (w_query.shape[1], w_key.shape[1], w_value.shape[1])
    pair_widths = (w_gate.shape[1], w_up.shape[1])
    inv_one = lax.rsqrt(jnp.mean(inputs * inputs, -1, keepdims=True) + EPS)
    unit_one = inputs * inv_one
    normed = (unit_one * gain_one).astype(jnp.bfloat16)
    joint = spread_columns(normed, jnp.concatenate(slabs[0:3], 1))
    query_portion, key_portion, v_part = split_lanes(joint, joint_widths, lanes)
    cosine_table, sine_table = rope_tables(q_pos.astype(jnp.float32), HEAD_SIZE // 2)
    query_heads = rotary_apply(
        (query_portion + query_bias_vector).reshape(
            token_rows, KEY_VALUE_HEADS, head_groups, HEAD_SIZE
        ),
        cosine_table,
        sine_table,
    ).astype(jnp.bfloat16)
    key_head_rows = rotary_apply(
        key_portion.reshape(token_rows, KEY_VALUE_HEADS, HEAD_SIZE), cosine_table, sine_table
    ).astype(jnp.bfloat16)
    value_heads = (v_part + bias_value).astype(jnp.bfloat16)
    gathered_keys, gathered_values = (
        lax.all_gather(
            key_head_rows.reshape(token_rows, KEY_VALUE_HEADS * HEAD_SIZE),
            "fsdp",
            axis=0,
            tiled=True,
        ),
        lax.all_gather(value_heads, "fsdp", axis=0, tiled=True),
    )
    key_block_slice = min(512, grouped_rows)
    block_count = grouped_rows // key_block_slice
    block_tiles = (
        gathered_keys.reshape(block_count, key_block_slice, KEY_VALUE_HEADS, HEAD_SIZE),
        gathered_values.reshape(block_count, key_block_slice, KEY_VALUE_HEADS, HEAD_SIZE),
        k_valid.reshape(block_count, key_block_slice),
        k_index.reshape(block_count, key_block_slice),
        k_seq.reshape(block_count, key_block_slice),
        group_slots.reshape(block_count, key_block_slice),
    )

    def scores(tile):
        raw = (
            jnp.einsum("qgjd,kgd->gjqk", query_heads, tile[0], preferred_element_type=jnp.float32)
            * scale
        )
        allowed = allowed_pairs(query_meta, (tile[2], tile[3], tile[4], tile[5]))
        return (jnp.where(allowed[None, None], raw, NEGATIVE_FILL), allowed)

    def stats(carry, tile):
        top, total = carry
        masked, allowed = scores(tile)
        new_top = jnp.maximum(top, jnp.max(masked, -1))
        shifted = jnp.where(allowed[None, None], jnp.exp(masked - new_top[..., None]), 0.0)
        total = total * jnp.exp(top - new_top) + jnp.sum(shifted, -1)
        return ((new_top, total), None)

    upper_start = jnp.full((KEY_VALUE_HEADS, head_groups, token_rows), NEGATIVE_FILL, jnp.float32)
    overall_start = jnp.zeros((KEY_VALUE_HEADS, head_groups, token_rows), jnp.float32)
    (top, total), unused_result = lax.scan(stats, (upper_start, overall_start), block_tiles)
    log_total = top + jnp.log(total)

    def weight_apply(acc, tile):
        masked, allowed = scores(tile)
        probs = jnp.exp(masked - log_total[..., None]).astype(jnp.bfloat16)
        return (
            acc + jnp.einsum("gjqk,kgd->qgjd", probs, tile[1], preferred_element_type=jnp.float32),
            None,
        )

    attention_heads, unused_result = lax.scan(
        weight_apply,
        jnp.zeros((token_rows, KEY_VALUE_HEADS, head_groups, HEAD_SIZE), jnp.float32),
        block_tiles,
    )
    heads_out = attention_heads.reshape(token_rows, QUERY_HEADS * HEAD_SIZE).astype(jnp.bfloat16)
    proj = spread_columns(heads_out, slabs[3])
    hidden = inputs + valid_col * proj
    inv_two = lax.rsqrt(jnp.mean(hidden * hidden, -1, keepdims=True) + EPS)
    unit_two = hidden * inv_two
    normed2 = (unit_two * gain_two).astype(jnp.bfloat16)
    paired = spread_columns(normed2, jnp.concatenate(slabs[4:6], 1))
    gate, up_val = split_lanes(paired, pair_widths, lanes)
    act = (jax.nn.silu(gate) * up_val).astype(jnp.bfloat16)
    down = spread_columns(act, slabs[6])
    mixed = (hidden + valid_col * down).astype(jnp.bfloat16)
    slabs_back = (
        lax.all_gather(matrices[0], "fsdp", axis=0, tiled=True),
        lax.all_gather(matrices[1], "fsdp", axis=0, tiled=True),
        lax.all_gather(matrices[2], "fsdp", axis=0, tiled=True),
        lax.all_gather(matrices[3], "fsdp", axis=0, tiled=True),
        lax.all_gather(matrices[4], "fsdp", axis=0, tiled=True),
        lax.all_gather(matrices[5], "fsdp", axis=0, tiled=True),
        lax.all_gather(matrices[6], "fsdp", axis=0, tiled=True),
    )
    grad_out = cotangent[0].astype(jnp.float32)
    d_down = (valid_col * grad_out).astype(jnp.bfloat16)
    d_act = fold_columns(d_down, slabs_back[6])
    sigma = jax.nn.sigmoid(gate)
    d_gate = (d_act * up_val * sigma * (1.0 + gate * (1.0 - sigma))).astype(jnp.bfloat16)
    d_up = (d_act * gate * sigma).astype(jnp.bfloat16)
    d_paired = alternate((d_gate, d_up), lanes)
    d_n2 = fold_columns(d_paired, jnp.concatenate(slabs_back[4:6], 1))
    scaled_two = d_n2 * gain_two
    dh = grad_out + inv_two * (
        scaled_two - unit_two * jnp.mean(scaled_two * unit_two, -1, keepdims=True)
    )
    grad_gain_two = jnp.sum(d_n2 * unit_two, 0)
    d_proj = (valid_col * dh).astype(jnp.bfloat16)
    head_gradient = fold_columns(d_proj, slabs_back[3]).astype(jnp.bfloat16)
    head_gradient4 = head_gradient.reshape(token_rows, KEY_VALUE_HEADS, head_groups, HEAD_SIZE)
    delta = jnp.einsum("qgjd,qgjd->gjq", head_gradient4.astype(jnp.float32), attention_heads)

    def attend_reverse(grad_query, tile):
        masked, allowed = scores(tile)
        probs = jnp.exp(masked - log_total[..., None])
        grad_value = jnp.einsum(
            "gjqk,qgjd->kgd",
            probs.astype(jnp.bfloat16),
            head_gradient4,
            preferred_element_type=jnp.float32,
        )
        grad_probs = jnp.einsum(
            "qgjd,kgd->gjqk", head_gradient4, tile[1], preferred_element_type=jnp.float32
        )
        grad_scores = (probs * (grad_probs - delta[..., None])).astype(jnp.bfloat16)
        grad_query = (
            grad_query
            + jnp.einsum("gjqk,kgd->qgjd", grad_scores, tile[0], preferred_element_type=jnp.float32)
            * scale
        )
        grad_key = (
            jnp.einsum(
                "gjqk,qgjd->kgd", grad_scores, query_heads, preferred_element_type=jnp.float32
            )
            * scale
        )
        return (grad_query, (grad_key, grad_value))

    grad_query, (key_gradient, value_gradient) = lax.scan(
        attend_reverse,
        jnp.zeros((token_rows, KEY_VALUE_HEADS, head_groups, HEAD_SIZE), jnp.float32),
        block_tiles,
    )
    local_keys, own_values = (
        lax.psum_scatter(
            key_gradient.reshape(grouped_rows, KEY_VALUE_HEADS * HEAD_SIZE).astype(jnp.bfloat16),
            "fsdp",
            scatter_dimension=0,
            tiled=True,
        ).astype(jnp.float32),
        lax.psum_scatter(
            value_gradient.reshape(grouped_rows, KEY_VALUE_HEADS * HEAD_SIZE).astype(jnp.bfloat16),
            "fsdp",
            scatter_dimension=0,
            tiled=True,
        ).astype(jnp.float32),
    )
    d_q_pre = (
        rotary_reverse(grad_query, cosine_table, sine_table)
        .reshape(token_rows, QUERY_HEADS * HEAD_SIZE)
        .astype(jnp.bfloat16)
    )
    d_k_pre = (
        rotary_reverse(
            local_keys.reshape(token_rows, KEY_VALUE_HEADS, HEAD_SIZE), cosine_table, sine_table
        )
        .reshape(token_rows, KEY_VALUE_HEADS * HEAD_SIZE)
        .astype(jnp.bfloat16)
    )
    d_v_pre = own_values.astype(jnp.bfloat16)
    d_joint = alternate((d_q_pre, d_k_pre, d_v_pre), lanes)
    d_n1 = fold_columns(d_joint, jnp.concatenate(slabs_back[0:3], 1))
    scaled_one = d_n1 * gain_one
    d_tokens = (
        dh + inv_one * (scaled_one - unit_one * jnp.mean(scaled_one * unit_one, -1, keepdims=True))
    ).astype(jnp.bfloat16)
    grad_gain_one = jnp.sum(d_n1 * unit_one, 0)
    local_vectors = jnp.concatenate(
        [
            grad_gain_one,
            jnp.sum(d_q_pre.astype(jnp.float32), 0),
            jnp.sum(d_v_pre.astype(jnp.float32), 0),
            grad_gain_two,
        ]
    )
    summed_vectors = lax.psum(local_vectors, ("fsdp", "dp"))
    dp_place = lax.axis_index("dp")
    sections = (attn_gain.shape[0], b_query.shape[0], b_value.shape[0], mlp_gain.shape[0])
    vector_pieces = []
    offset = 0
    for width in sections:
        whole_width = width * lanes
        vector_pieces.append(
            lax.dynamic_slice_in_dim(summed_vectors, offset + dp_place * width, width)
        )
        offset = offset + whole_width
    joint_grad, out_grad, pair_grad, down_grad = weight_grads(
        ((normed, d_joint), (heads_out, d_proj), (normed2, d_paired), (act, d_down))
    )
    first_cut = joint_widths[0]
    second_cut = joint_widths[0] + joint_widths[1]
    grad_w_query = joint_grad[:, :first_cut]
    grad_w_key = joint_grad[:, first_cut:second_cut]
    grad_w_value = joint_grad[:, second_cut:]
    grad_w_gate = pair_grad[:, : pair_widths[0]]
    grad_w_up = pair_grad[:, pair_widths[0] :]
    return (
        mixed[None],
        d_tokens[None],
        vector_pieces[0],
        grad_w_query,
        vector_pieces[1],
        grad_w_key,
        grad_w_value,
        vector_pieces[2],
        out_grad,
        vector_pieces[3],
        grad_w_gate,
        grad_w_up,
        down_grad,
    )


def solution(mesh):
    placed = (
        P("dp", "fsdp", None),
        P("dp", "fsdp", None),
        P("dp", None),
        P("dp", None),
        P("dp"),
        P("fsdp", "dp"),
        P("dp"),
        P("fsdp", "dp"),
        P("fsdp", "dp"),
        P("dp"),
        P("fsdp", "dp"),
        P("dp"),
        P("fsdp", "dp"),
        P("fsdp", "dp"),
        P("fsdp", "dp"),
    )
    return jax.shard_map(
        body,
        mesh=mesh,
        in_specs=placed,
        out_specs=(
            P("dp", "fsdp", None),
            P("dp", "fsdp", None),
            P("dp"),
            P("fsdp", "dp"),
            P("dp"),
            P("fsdp", "dp"),
            P("fsdp", "dp"),
            P("dp"),
            P("fsdp", "dp"),
            P("dp"),
            P("fsdp", "dp"),
            P("fsdp", "dp"),
            P("fsdp", "dp"),
        ),
        check_vma=False,
    )
```

profile of v0, /device:TPU:0, one launch (start us, length us, event | category | flops | bytes accessed | tf_op | source)
XLA Modules:
  0.0 903.4 jit_solution(1251615326101400332)
XLA Ops:
  9.5 15.1 %all-gather.1 = bf16[4,224,16]{1,2,0:T(8,128)(2,1)S(1)} all-gather(bf16[1,224,16]{1,2,0:T(8,128)(2,1)} %bitcast.392), channel_id=1, replica_groups=mesh['fsdp'=4,'dp'=8] {'fsdp'}, dimensions={0}, use_global_device_ids=true | all-gather | bytes 35840 | tf_op jit(solution)/shard_map/all_gather | solution.py:179
  24.7 13.5 %all-gather = bf16[4,224,16]{1,2,0:T(8,128)(2,1)S(1)} all-gather(bf16[1,224,16]{1,2,0:T(8,128)(2,1)} %bitcast.393), channel_id=1, replica_groups=mesh['fsdp'=4,'dp'=8] {'fsdp'}, dimensions={0}, use_global_device_ids=true | all-gather | bytes 35840 | tf_op jit(solution)/shard_map/all_gather | solution.py:178
  38.3 14.6 %all_gather.63 = bf16[896,112]{1,0:T(8,128)(2,1)S(1)} all-gather(bf16[224,112]{1,0:T(8,128)(2,1)} %param.26), channel_id=1, replica_groups=mesh['fsdp'=4,'dp'=8] {'fsdp'}, dimensions={0}, use_global_device_ids=true | all-gather | bytes 250880 | tf_op jit(solution)/shard_map/all_gather | solution.py:177
  54.1 15.2 %all_gather.71 = bf16[896,112]{1,0:T(8,128)(2,1)S(1)} all-gather(bf16[224,112]{1,0:T(8,128)(2,1)S(1)} %copy-done.27), channel_id=1, replica_groups=mesh['fsdp'=4,'dp'=8] {'fsdp'}, dimensions={0}, use_global_device_ids=true | all-gather | bytes 250880 | tf_op jit(solution)/shard_map/all_gather | solution.py:180
  85.7 14.6 %all-reduce.4 = (bf16[896]{0:T(1024)(128)(2,1)S(1)}, bf16[896]{0:T(1024)(128)(2,1)S(1)}, bf16[128]{0:T(256)(128)(2,1)S(1)}, bf16[896]{0:T(1024)(128)(2,1)S(1)}) all-reduce(bf16[896]{0:T(1024)(128)(2,1)S(1)} %dynamic-update-slice.2, bf16[896]{0:T(1024)(128)(2,1)S(1)} %dynamic-update-slice, ...), channel_id=1, replica_groups=mesh['fsdp'=4,'dp'=8] {'dp'}, use_global_device_ids=true, to_apply=%add.2 | all-reduce | flops 2816 | bytes 11264
  111.5 25.9 %all-gather.11.cloned.1.call-done = bf16[896,1152]{0,1:T(8,128)(2,1)} async-done(((bf16[896,144]{0,1:T(8,128)(2,1)}), bf16[896,1152]{0,1:T(8,128)(2,1)}) %all-gather.11.cloned.1.call-update) | async-done | bytes 2064400 | tf_op jit(solution)/shard_map/all_gather | solution.py:101
  141.2 14.8 %all_gather.68 = bf16[1536,128]{0,1:T(8,128)(2,1)S(1)} all-gather(bf16[384,128]{0,1:T(8,128)(2,1)S(1)} %fusion.103), channel_id=1, replica_groups=mesh['fsdp'=4,'dp'=8] {'fsdp'}, dimensions={0}, use_global_device_ids=true | all-gather | bytes 491520 | tf_op jit(solution)/shard_map/all_gather | solution.py:211
  157.4 16.4 %all_gather.69 = bf16[1536,128]{0,1:T(8,128)(2,1)} all-gather(bf16[384,128]{0,1:T(8,128)(2,1)S(1)} %fusion.100), channel_id=1, replica_groups=mesh['fsdp'=4,'dp'=8] {'fsdp'}, dimensions={0}, use_global_device_ids=true | all-gather | bytes 491520 | tf_op jit(solution)/shard_map/all_gather | solution.py:205
  178.8 42.4 %while.39 = (s32[]{:T(128)}, f32[2,7,384]{2,1,0:T(8,128)S(1)}, f32[2,7,384]{2,1,0:T(8,128)S(1)}, s32[384]{0:T(512)S(1)}, s32[3,512]{1,0:T(4,128)S(1)}, /*index=5...) while((s32[]{:T(128)}, f32[2,7,384]{2,1,0:T(8,128)S(1)}, ...), condition=%wide.region_10.11_spmd.clone, body=%wide.region_7.10_spmd.clone.sunk | while | flops 375744768 | bytes 23733808 | solution.py:242
  221.3 19.9 %while.40 = (s32[]{:T(128)}, f32[384,2,7,64]{0,3,2,1:T(8,128)}, bf16[3,512,2,64]{1,3,2,0:T(8,128)(2,1)}, s32[384]{0:T(512)S(1)}, s32[3,512]{1,0:T(4,128)S(1)}, /...) while((s32[]{:T(128)}, f32[384,2,7,64]{0,3,2,1:T(8,128)}, ...), condition=%wide.region_12.13_spmd.clone, body=%wide.region_11.12_spmd.clone.sunk | while | flops 717717504 | bytes 4147250 | solution.py:253
  247.3 12.7 %all-gather.19.cloned.1.call-done = bf16[896,9728]{0,1:T(8,128)(2,1)} async-done(((bf16[896,1216]{0,1:T(8,128)(2,1)}), bf16[896,9728]{0,1:T(8,128)(2,1)}) %all-gather.19.cloned.1.call-update) | async-done | bytes 17432592 | tf_op jit(solution)/shard_map/all_gather | solution.py:101
  260.0 17.5 %fusion.119 = f32[384,9728]{0,1:T(8,128)} fusion(bf16[896,9728]{0,1:T(8,128)(2,1)} %all-gather.19.cloned.1.call-done, f32[384,896]{1,0:T(8,128)} %get-tuple-element.816, f32[896]{0:T(1024)S(1)} %convert_element_type.184, f32[384]{0:T(512)S(1)} %add_rsqrt_fusion), kind=kOutput, calls=%fused_computation.200 | convolution fusion | flops 6695141376 | bytes 33756160 | tf_op jit(solution)/shard_map/dot_general | solution.py:100
  317.7 12.3 %multiply_convert_fusion.2 = (bf16[384,4864]{1,0:T(8,128)(2,1)}, bf16[384,4864]{1,0:T(8,128)(2,1)}) fusion(f32[384,4864]{1,0:T(8,128)} %copy.151, f32[384,4864]{1,0:T(8,128)} %copy.152, bf16[4864,896]{0,1:T(8,128)(2,1)} %all-gather.21.cloned.1.call-done, bf16[1,384,896]{2,1,0:T(8,128)(2,1)S(1)} %copy-done.17, f32[384]{0:T(512)S(1)} %get-tuple-element.776), kind=kOutput, calls=%fused_computation.76 | convolution fusion | flops 3372367872 | bytes 31819264 | tf_op jit(solution)/shard_map/dot_general | solution.py:106
  349.2 15.8 %multiply_reduce_fusion = (f32[896]{0:T(1024)}, f32[384]{0:T(512)S(1)}, f32[384,896]{1,0:T(8,128)S(1)}) fusion(f32[384,896]{1,0:T(8,128)S(1)} %copy-done.16, f32[384]{0:T(512)S(1)} %add_rsqrt_fusion, f32[896]{0:T(1024)S(1)} %convert_element_type.184, bf16[384,9728]{0,1:T(8,128)(2,1)} %bitcast.358, bf16[896,9728]{0,1:T(8,128)(2,1)} %all-gather.19.cloned.1.call-done), kind=kOutput, calls=%fused_computation.116 | convolution fusion | flops 6696172032 | bytes 27666432 | tf_op jit(solution)/shard_map/dot_general | solution.py:106
  371.5 68.0 %while.41 = (s32[]{:T(128)}, f32[384,2,7,64]{0,3,2,1:T(8,128)S(1)}, bf16[3,512,2,64]{1,3,2,0:T(8,128)(2,1)}, bf16[3,512,2,64]{1,3,2,0:T(8,128)(2,1)}, bf16[3,512...) while((s32[]{:T(128)}, f32[384,2,7,64]{0,3,2,1:T(8,128)S(1)}, ...), condition=%wide.region_16.17_spmd.clone, body=%wide.region_15.16_spmd.clone.sunk | while | flops 1791606784 | bytes 129002256 | solution.py:322
  451.1 12.4 %reduce-scatter.31.cloned.1.call-done = bf16[384,128]{1,0:T(8,128)(2,1)} async-done(((bf16[1536,128]{1,0:T(8,128)(2,1)}), bf16[384,128]{1,0:T(8,128)(2,1)}) %reduce-scatter.31.cloned.1.call-update) | async-done | bytes 98320
  465.6 19.8 %reduce-scatter.33.cloned.1.call-done = bf16[384,128]{1,0:T(8,128)(2,1)} async-done(((bf16[1536,128]{1,0:T(8,128)(2,1)}), bf16[384,128]{1,0:T(8,128)(2,1)}) %reduce-scatter.33.cloned.1.call-update) | async-done | bytes 98320
  502.4 16.1 %convolution_convert_fusion = bf16[9728,896]{1,0:T(8,128)(2,1)} fusion(bf16[384,9728]{0,1:T(8,128)(2,1)} %bitcast.359, f32[384,896]{1,0:T(8,128)} %get-tuple-element.816, f32[896]{0:T(1024)S(1)} %convert_element_type.184, f32[384]{0:T(512)S(1)} %copy-done.29), kind=kOutput, calls=%fused_computation.71 | convolution fusion | flops 6703857664 | bytes 26285056 | tf_op jit(solution)/shard_map/dot_general | solution.py:116
  527.4 42.7 %reduce-scatter.23.cloned.1.call-done = bf16[144,896]{1,0:T(8,128)(2,1)} async-done(((bf16[1152,896]{1,0:T(8,128)(2,1)}), bf16[144,896]{1,0:T(8,128)(2,1)}) %reduce-scatter.23.cloned.1.call-update) | async-done | bytes 258064 | tf_op jit(solution)/shard_map/reduce_scatter | solution.py:115
  572.2 74.4 %reduce-scatter.29.cloned.1.call-done = bf16[112,4864]{1,0:T(8,128)(2,1)} async-done(((bf16[896,4864]{1,0:T(8,128)(2,1)}), bf16[112,4864]{1,0:T(8,128)(2,1)}) %reduce-scatter.29.cloned.1.call-update) | async-done | bytes 1089552 | tf_op jit(solution)/shard_map/reduce_scatter | solution.py:115
  649.3 120.1 %reduce-scatter.27.cloned.1.call-done = bf16[1216,896]{1,0:T(8,128)(2,1)} async-done(((bf16[9728,896]{1,0:T(8,128)(2,1)}), bf16[1216,896]{1,0:T(8,128)(2,1)}) %reduce-scatter.27.cloned.1.call-update) | async-done | bytes 2179088 | tf_op jit(solution)/shard_map/reduce_scatter | solution.py:115
  773.7 13.2 %fusion.88 = bf16[1,384,896]{2,1,0:T(8,128)(2,1)} fusion(f32[384,896]{1,0:T(8,128)} %get-tuple-element.816, bf16[4864,896]{0,1:T(8,128)(2,1)} %all-gather.21.cloned.1.call-done, f32[384,4864]{1,0:T(8,128)} %copy.152, f32[384,4864]{1,0:T(8,128)} %copy.151, f32[384]{0:T(512)S(1)} %get-tuple-element.776), kind=kOutput, calls=%fused_computation.124 | convolution fusion | flops 3359293440 | bytes 25724416 | tf_op jit(solution)/shard_map/dot_general | solution.py:100
  789.4 39.9 %psum.7 = f32[2816]{0:T(1024)S(1)} all-reduce(f32[2816]{0:T(1024)S(1)} %pad_maximum_fusion.7), channel_id=1, replica_groups=mesh['fsdp'=4,'dp'=8] {'fsdp','dp'}, use_global_device_ids=true, to_apply=%region_24.25 | all-reduce | flops 2816 | bytes 22528 | tf_op jit(solution)/shard_map/psum | solution.py:369
  846.7 46.1 %reduce-scatter.39.cloned.1.call-done = bf16[224,1216]{1,0:T(8,128)(2,1)} async-done(((bf16[896,1216]{1,0:T(8,128)(2,1)}), bf16[224,1216]{1,0:T(8,128)(2,1)}) %reduce-scatter.39.cloned.1.call-update) | async-done | bytes 544784
  (340 shorter events, 313.3 us)
Async XLA Ops:
  7.2 63.1 %all-gather.17.cloned.1.call-start = ((), (), s32[]{:S(2)}) async-start(), calls=%async_computation.13 | async-start | bytes 1433600 | tf_op jit(solution)/shard_map/all_gather | solution.py:182
  7.9 46.2 %copy-start.27 = (bf16[224,112]{1,0:T(8,128)(2,1)S(1)}, bf16[224,112]{1,0:T(8,128)(2,1)}, u32[]{:S(2)}) copy-start(bf16[224,112]{1,0:T(8,128)(2,1)} %param.31) | copy-start | bytes 150532
  7.9 69.2 %all-gather.15.cloned.1.call-start = ((), (), s32[]{:S(2)}) async-start(), calls=%async_computation.12 | async-start | bytes 1433600 | tf_op jit(solution)/shard_map/all_gather | solution.py:181
  8.7 99.2 %all-gather.23.cloned.1.call-start = ((), (), s32[]{:S(2)}) async-start(), calls=%async_computation.20 | async-start | bytes 1433600 | tf_op jit(solution)/shard_map/all_gather | solution.py:183
  9.4 128.1 %all-gather.11.cloned.1.call-start = ((), (), s32[]{:S(2)}) async-start(), calls=%async_computation.10 | async-start | bytes 2322432 | tf_op jit(solution)/shard_map/all_gather | solution.py:101
  54.1 189.4 %all-gather.13.cloned.1.call-start = ((), (), s32[]{:S(2)}) async-start(), calls=%async_computation.11 | async-start | bytes 1806336 | tf_op jit(solution)/shard_map/all_gather | solution.py:101
  70.2 189.9 %all-gather.19.cloned.1.call-start = ((), (), s32[]{:S(2)}) async-start(), calls=%async_computation.14 | async-start | bytes 19611648 | tf_op jit(solution)/shard_map/all_gather | solution.py:101
  82.3 235.5 %all-gather.21.cloned.1.call-start = ((), (), s32[]{:S(2)}) async-start(), calls=%async_computation.15 | async-start | bytes 9805824 | tf_op jit(solution)/shard_map/all_gather | solution.py:101
  100.3 37.2 %copy-start.25 = (f32[896]{0:T(1024)}, f32[896]{0:T(1024)S(1)}, u32[]{:S(2)}) copy-start(f32[896]{0:T(1024)S(1)} %convert_element_type.173) | copy-start | bytes 10756
  102.1 53.9 %copy-start.12 = (f32[384,64]{0,1:T(8,128)}, f32[384,64]{0,1:T(8,128)S(1)}, u32[]{:S(2)}) copy-start(f32[384,64]{0,1:T(8,128)S(1)} %get-tuple-element.820) | copy-start | bytes 294916
  102.1 76.2 %copy-start.10 = (f32[384,64]{0,1:T(8,128)}, f32[384,64]{0,1:T(8,128)S(1)}, u32[]{:S(2)}) copy-start(f32[384,64]{0,1:T(8,128)S(1)} %get-tuple-element.819) | copy-start | bytes 294916
  102.4 35.1 %copy-start.23 = (f32[384]{0:T(512)}, f32[384]{0:T(512)S(1)}, u32[]{:S(2)}) copy-start(f32[384]{0:T(512)S(1)} %add_rsqrt_fusion.1) | copy-start | bytes 4612
  111.5 351.9 %reduce-scatter.31.cloned.1.call-start = ((), (), s32[]{:S(2)}) async-start(), calls=%async_computation.21 | async-start | bytes 491520
  247.3 117.8 %copy-start.28 = (f32[384]{0:T(512)}, f32[384]{0:T(512)S(1)}, u32[]{:S(2)}) copy-start(f32[384]{0:T(512)S(1)} %add_rsqrt_fusion) | copy-start | bytes 4612
  442.7 42.6 %reduce-scatter.33.cloned.1.call-start = ((), (), s32[]{:S(2)}) async-start(), calls=%async_computation.22 | async-start | bytes 491520
  446.2 79.4 %reduce-scatter.25.cloned.1.call-start = ((), (), s32[]{:S(2)}) async-start(), calls=%async_computation.17 | async-start | bytes 1806336 | tf_op jit(solution)/shard_map/reduce_scatter | solution.py:115
  449.7 120.5 %reduce-scatter.23.cloned.1.call-start = ((), (), s32[]{:S(2)}) async-start(), calls=%async_computation.16 | async-start | bytes 2322432 | tf_op jit(solution)/shard_map/reduce_scatter | solution.py:115
  464.5 22.9 %copy-start.7 = (bf16[1,384,896]{2,1,0:T(8,128)(2,1)S(1)}, bf16[1,384,896]{2,1,0:T(8,128)(2,1)}, u32[]{:S(2)}) copy-start(bf16[1,384,896]{2,1,0:T(8,128)(2,1)} %param.21) | copy-start | bytes 2064388
  490.2 156.4 %reduce-scatter.29.cloned.1.call-start = ((), (), s32[]{:S(2)}) async-start(), calls=%async_computation.19 | async-start | bytes 9805824 | tf_op jit(solution)/shard_map/reduce_scatter | solution.py:115
  501.8 267.7 %reduce-scatter.27.cloned.1.call-start = ((), (), s32[]{:S(2)}) async-start(), calls=%async_computation.18 | async-start | bytes 19611648 | tf_op jit(solution)/shard_map/reduce_scatter | solution.py:115
  518.5 314.5 %reduce-scatter.37.cloned.1.call-start = ((), (), s32[]{:S(2)}) async-start(), calls=%async_computation.24 | async-start | bytes 286720
  527.4 307.3 %reduce-scatter.35.cloned.1.call-start = ((), (), s32[]{:S(2)}) async-start(), calls=%async_computation.23 | async-start | bytes 573440
  572.1 272.6 %reduce-scatter.41.cloned.1.call-start = ((), (), s32[]{:S(2)}) async-start(), calls=%async_computation.26 | async-start | bytes 1556480
  649.0 243.9 %reduce-scatter.39.cloned.1.call-start = ((), (), s32[]{:S(2)}) async-start(), calls=%async_computation.25 | async-start | bytes 2867200
  (45 other events, 282.4 us)
Sparse Core Ops, SparseCore 0:
  9.6 34.5 all-gather.16
  45.7 31.2 all-gather.14
  78.7 29.1 all-gather.22
  110.2 27.2 all-gather.10
  139.8 25.8 all-gather.12
  167.4 92.6 all-gather.18
  261.9 55.7 all-gather.20
  442.8 20.5 reduce-scatter.30
  466.4 18.8 reduce-scatter.32
  488.6 36.9 reduce-scatter.24
  529.4 40.7 reduce-scatter.22
  573.6 72.9 reduce-scatter.28
  650.2 119.2 reduce-scatter.26
  772.2 19.5 reduce-scatter.36
  794.5 19.6 reduce-scatter.34
  816.4 28.3 reduce-scatter.40
  847.0 45.7 reduce-scatter.38
where the time goes:
time: 911 us; the launch traced here: 903 us
  waiting for transfers between devices  395 us (43%)
  matrix products  203 us (22%)
  blocking collectives  144 us (16%)
  local copies, waits for them, and re-layouts  81.9 us (9%)
  other arithmetic  61.4 us (7%)
  between operations  16.5 us (2%)
    reduce_scatter x4, waiting for transfers between devices, column_terms(): lax.psum_scatter(lax.dot_general(grad, left, (((0,), (0,)), ((), ())), pr...  244 us
    unnamed x23, waiting for transfers between devices  88.2 us
    all_gather x4, waiting for transfers between devices, spread_columns(): lax.all_gather(slab, 'dp', axis=1, tiled=True)  50.6 us
    psum x1, blocking collectives, body(): summed_vectors = lax.psum(local_vectors, ('fsdp', 'dp'))  39.9 us
    dot_general x4, matrix products, spread_columns(): jnp.dot(left, lax.all_gather(slab, 'dp', axis=1, tiled=True), preferred_e...  37.5 us
    unnamed x100, local copies, waits for them, and re-layouts  36.7 us
    dot_general x4, matrix products, column_terms(): lax.dot_general(grad, left, (((0,), (0,)), ((), ())), preferred_element_t...  32.8 us
    dot_general x4, matrix products, fold_columns(): lax.dot_general(grad, lax.all_gather(slab, 'dp', axis=1, tiled=True), (((...  32.4 us
  transfers between devices with their start and end apart: 17, of which 13 were waited for; matrix products, arithmetic and copies ran while one was open for 24% of the time, Pallas kernels for 0%

commit v1 on v0

--- a/solution.py
+++ b/solution.py
@@ -78,57 +78,99 @@
     return tensor * cosine_table.reshape(shape) + turned
 
 
-def alternate(parts, lanes):
-    token_count = parts[0].shape[0]
-    return jnp.concatenate([p.reshape(token_count, lanes, -1) for p in parts], 2).reshape(
-        token_count, -1
-    )
-
-
-def split_lanes(whole, widths, lanes):
-    token_count = whole.shape[0]
-    cube = whole.reshape(token_count, lanes, -1)
-    pieces = []
-    offset = 0
-    for width in widths:
-        pieces.append(cube[:, :, offset : offset + width].reshape(token_count, -1))
-        offset = offset + width
-    return pieces
-
-
-def spread_columns(left, slab):
-    return jnp.dot(
-        left, lax.all_gather(slab, "dp", axis=1, tiled=True), preferred_element_type=jnp.float32
-    )
-
-
-def fold_columns(grad, slab):
+def flip(array, mask, size):
+    return lax.ppermute(array, "dp", [(i, i ^ mask) for i in range(size)])
+
+
+def gather_tokens(rows, size):
+    if size != 8:
+        return lax.all_gather(rows, "dp", axis=0)
+    half = rows.shape[0] // 2
+    by_x, by_y, by_core = flip(rows, 2, 8), flip(rows, 4, 8), flip(rows, 1, 8)
+    far_a, far_b = flip(by_x[:half], 4, 8), flip(by_y[half:], 2, 8)
+    core_x, core_y = flip(by_x, 1, 8), flip(by_y, 1, 8)
+    core_a, core_b = flip(far_a, 1, 8), flip(far_b, 1, 8)
+    return jnp.stack(
+        [
+            rows,
+            by_core,
+            by_x,
+            core_x,
+            by_y,
+            core_y,
+            jnp.concatenate([far_a, far_b]),
+            jnp.concatenate([core_a, core_b]),
+        ]
+    )
+
+
+def scatter_tokens(parts, size):
+    if size != 8:
+        return lax.psum_scatter(
+            parts.astype(jnp.bfloat16), "dp", scatter_dimension=0, tiled=False
+        ).astype(jnp.float32)
+    sent = parts.astype(jnp.bfloat16)
+    half = parts.shape[1] // 2
+    wide = jnp.float32
+    seven, five, three, one = [flip(sent[k], 1, 8) for k in (7, 5, 3, 1)]
+    far = (parts[6].astype(wide) + seven.astype(wide)).astype(jnp.bfloat16)
+    far_x, far_y = flip(far[:half], 2, 8), flip(far[half:], 4, 8)
+    on_y = parts[4].astype(wide) + five.astype(wide)
+    on_x = parts[2].astype(wide) + three.astype(wide)
+    on_y = jnp.concatenate([on_y[:half] + far_x.astype(wide), on_y[half:]]).astype(jnp.bfloat16)
+    on_x = jnp.concatenate([on_x[:half], on_x[half:] + far_y.astype(wide)]).astype(jnp.bfloat16)
+    got_x, got_y = flip(on_x, 2, 8), flip(on_y, 4, 8)
+    own = parts[0].astype(wide) + one.astype(wide)
+    return own + got_x.astype(wide) + got_y.astype(wide)
+
+
+def exchange(parts, size):
+    if size != 8:
+        return lax.all_to_all(parts, "dp", 0, 0, tiled=True)
+    place = lax.axis_index("dp")
+    result = parts
+    for k in range(1, 8):
+        piece = flip(lax.dynamic_index_in_dim(parts, place ^ k, 0, True), k, 8)
+        result = lax.dynamic_update_slice_in_dim(result, piece, place ^ k, 0)
+    return result
+
+
+def gather_rows(rows, size):
+    place = lax.axis_index("fsdp")
+    result = jnp.zeros((size,) + rows.shape, rows.dtype)
+    result = lax.dynamic_update_slice_in_dim(result, rows[None], place, 0)
+    for k in range(1, size):
+        piece = lax.ppermute(rows, "fsdp", [(i, (i + k) % size) for i in range(size)])
+        result = lax.dynamic_update_slice_in_dim(result, piece[None], (place + size - k) % size, 0)
+    return result
+
+
+def scatter_rows(parts, size):
+    place = lax.axis_index("fsdp")
+    sent = parts.astype(jnp.bfloat16)
+    total = lax.dynamic_index_in_dim(parts, place, 0, False).astype(jnp.float32)
+    for k in range(1, size):
+        piece = lax.dynamic_index_in_dim(sent, (place + k) % size, 0, False)
+        total = total + lax.ppermute(
+            piece, "fsdp", [(i, (i + k) % size) for i in range(size)]
+        ).astype(jnp.float32)
+    return total
+
+
+def dot_tn(left, right):
     return lax.dot_general(
-        grad,
-        lax.all_gather(slab, "dp", axis=1, tiled=True),
-        (((1,), (1,)), ((), ())),
-        preferred_element_type=jnp.float32,
-    )
-
-
-def column_terms(left, grad):
-    return lax.psum_scatter(
-        lax.dot_general(
-            grad, left, (((0,), (0,)), ((), ())), preferred_element_type=jnp.float32
-        ).astype(jnp.bfloat16),
-        "dp",
-        scatter_dimension=0,
-        tiled=True,
-    ).astype(jnp.float32)
-
-
-def weight_grads(pairs):
-    terms = tuple((column_terms(left, grad) for left, grad in pairs))
-    summed = jax.tree.map(
-        lambda part: part.astype(jnp.float32),
-        lax.psum_scatter(shortened(terms), "fsdp", scatter_dimension=1, tiled=True),
-    )
-    return tuple((jnp.transpose(s) for s in summed))
+        left, right, (((0,), (0,)), ((), ())), preferred_element_type=jnp.float32
+    )
+
+
+def dot_nt(left, right):
+    return lax.dot_general(
+        left, right, (((1,), (1,)), ((), ())), preferred_element_type=jnp.float32
+    )
+
+
+def dot_nn(left, right):
+    return jnp.dot(left, right, preferred_element_type=jnp.float32)
 
 
 def body(
@@ -165,30 +207,53 @@
     q_slot = lax.dynamic_slice_in_dim(group_slots, own_start, token_rows)
     query_meta = (q_valid, q_index, q_seq, q_slot)
     valid_col = q_valid.astype(jnp.float32)[:, None]
-    vectors = (
-        lax.all_gather(attn_gain, "dp", axis=0, tiled=True),
-        lax.all_gather(b_query, "dp", axis=0, tiled=True),
-        lax.all_gather(b_value, "dp", axis=0, tiled=True),
-        lax.all_gather(mlp_gain, "dp", axis=0, tiled=True),
-    )
-    gain_one, query_bias_vector, bias_value, gain_two = [v.astype(jnp.float32) for v in vectors]
-    matrices = (w_query, w_key, w_value, w_out, w_gate, w_up, w_down)
-    slabs = (
-        lax.all_gather(matrices[0], "fsdp", axis=0, tiled=True),
-        lax.all_gather(matrices[1], "fsdp", axis=0, tiled=True),
-        lax.all_gather(matrices[2], "fsdp", axis=0, tiled=True),
-        lax.all_gather(matrices[3], "fsdp", axis=0, tiled=True),
-        lax.all_gather(matrices[4], "fsdp", axis=0, tiled=True),
-        lax.all_gather(matrices[5], "fsdp", axis=0, tiled=True),
-        lax.all_gather(matrices[6], "fsdp", axis=0, tiled=True),
-    )
-    joint_widths = (w_query.shape[1], w_key.shape[1], w_value.shape[1])
-    pair_widths = (w_gate.shape[1], w_up.shape[1])
+    fsdp_size = lax.axis_size("fsdp")
+    width = tokens.shape[2]
+    query_part, key_part, out_part = w_query.shape[1], w_key.shape[1], w_out.shape[1]
+    hidden_part = w_gate.shape[1]
+    pieces_each = lanes // fsdp_size
+    vector_widths = (query_part, query_part, key_part, query_part)
+    projections = lax.all_gather(
+        jnp.concatenate([w_query, w_key, w_value, w_out], 1), "fsdp", axis=0, tiled=True
+    ).T
+    joint_rows = projections.shape[0]
+    vector_row = jnp.concatenate([attn_gain, b_query, b_value, mlp_gain])
+    vector_count = vector_row.shape[0]
+    vector_block = jnp.zeros((16, width), jnp.bfloat16).at[0, :vector_count].set(vector_row)
+    spread = lax.all_gather(jnp.concatenate([projections, vector_block]), "dp", axis=0)
+    edges = (0, query_part, query_part + key_part, query_part + 2 * key_part, joint_rows)
+    wq_t, wk_t, wv_t, wo_t = [
+        spread[:, edges[i] : edges[i + 1]].reshape(-1, width) for i in range(4)
+    ]
+    joint_t = jnp.concatenate([wq_t, wk_t, wv_t])
+    vector_table = spread[:, joint_rows, :vector_count].astype(jnp.float32)
+    marks = [0]
+    for size in vector_widths:
+        marks.append(marks[-1] + size)
+    gain_one, query_bias_vector, bias_value, gain_two = [
+        vector_table[:, marks[i] : marks[i + 1]].reshape(-1) for i in range(4)
+    ]
+    down_t = w_down.T.reshape(out_part, pieces_each, hidden_part).transpose(1, 0, 2)
+    hidden_slabs = lax.all_gather(
+        jnp.concatenate([w_gate, w_up, down_t.reshape(-1, hidden_part)]), "fsdp", axis=0
+    )
+    rows_each = w_gate.shape[0]
+    gate_w = hidden_slabs[:, :rows_each].reshape(width, hidden_part)
+    up_w = hidden_slabs[:, rows_each : 2 * rows_each].reshape(width, hidden_part)
+    down_w = exchange(
+        hidden_slabs[:, 2 * rows_each :].reshape(lanes, out_part, hidden_part), lanes
+    ).reshape(width, hidden_part)
+    grad_out = cotangent[0].astype(jnp.float32)
+    d_down = (valid_col * grad_out).astype(jnp.bfloat16)
+    d_down_all = gather_tokens(d_down, lanes).reshape(-1, width)
     inv_one = lax.rsqrt(jnp.mean(inputs * inputs, -1, keepdims=True) + EPS)
     unit_one = inputs * inv_one
     normed = (unit_one * gain_one).astype(jnp.bfloat16)
-    joint = spread_columns(normed, jnp.concatenate(slabs[0:3], 1))
-    query_portion, key_portion, v_part = split_lanes(joint, joint_widths, lanes)
+    joint = dot_nt(normed, joint_t)
+    query_width, key_width = QUERY_HEADS * HEAD_SIZE, KEY_VALUE_HEADS * HEAD_SIZE
+    query_portion = joint[:, :query_width]
+    key_portion = joint[:, query_width : query_width + key_width]
+    v_part = joint[:, query_width + key_width :]
     cosine_table, sine_table = rope_tables(q_pos.astype(jnp.float32), HEAD_SIZE // 2)
     query_heads = rotary_apply(
         (query_portion + query_bias_vector).reshape(
@@ -201,15 +266,14 @@
         key_portion.reshape(token_rows, KEY_VALUE_HEADS, HEAD_SIZE), cosine_table, sine_table
     ).astype(jnp.bfloat16)
     value_heads = (v_part + bias_value).astype(jnp.bfloat16)
-    gathered_keys, gathered_values = (
-        lax.all_gather(
-            key_head_rows.reshape(token_rows, KEY_VALUE_HEADS * HEAD_SIZE),
-            "fsdp",
-            axis=0,
-            tiled=True,
+    gathered = gather_rows(
+        jnp.concatenate(
+            [key_head_rows.reshape(token_rows, KEY_VALUE_HEADS * HEAD_SIZE), value_heads], 1
         ),
-        lax.all_gather(value_heads, "fsdp", axis=0, tiled=True),
-    )
+        fsdp_size,
+    ).reshape(grouped_rows, 2 * KEY_VALUE_HEADS * HEAD_SIZE)
+    gathered_keys = gathered[:, : KEY_VALUE_HEADS * HEAD_SIZE]
+    gathered_values = gathered[:, KEY_VALUE_HEADS * HEAD_SIZE :]
     key_block_slice = min(512, grouped_rows)
     block_count = grouped_rows // key_block_slice
     block_tiles = (
@@ -256,40 +320,66 @@
         block_tiles,
     )
     heads_out = attention_heads.reshape(token_rows, QUERY_HEADS * HEAD_SIZE).astype(jnp.bfloat16)
-    proj = spread_columns(heads_out, slabs[3])
+    proj = dot_nt(heads_out, wo_t)
     hidden = inputs + valid_col * proj
     inv_two = lax.rsqrt(jnp.mean(hidden * hidden, -1, keepdims=True) + EPS)
     unit_two = hidden * inv_two
     normed2 = (unit_two * gain_two).astype(jnp.bfloat16)
-    paired = spread_columns(normed2, jnp.concatenate(slabs[4:6], 1))
-    gate, up_val = split_lanes(paired, pair_widths, lanes)
-    act = (jax.nn.silu(gate) * up_val).astype(jnp.bfloat16)
-    down = spread_columns(act, slabs[6])
-    mixed = (hidden + valid_col * down).astype(jnp.bfloat16)
-    slabs_back = (
-        lax.all_gather(matrices[0], "fsdp", axis=0, tiled=True),
-        lax.all_gather(matrices[1], "fsdp", axis=0, tiled=True),
-        lax.all_gather(matrices[2], "fsdp", axis=0, tiled=True),
-        lax.all_gather(matrices[3], "fsdp", axis=0, tiled=True),
-        lax.all_gather(matrices[4], "fsdp", axis=0, tiled=True),
-        lax.all_gather(matrices[5], "fsdp", axis=0, tiled=True),
-        lax.all_gather(matrices[6], "fsdp", axis=0, tiled=True),
-    )
-    grad_out = cotangent[0].astype(jnp.float32)
-    d_down = (valid_col * grad_out).astype(jnp.bfloat16)
-    d_act = fold_columns(d_down, slabs_back[6])
+    normed2_all = gather_tokens(normed2, lanes).reshape(-1, width)
+    gate = dot_nn(normed2_all, gate_w)
+    up_val = dot_nn(normed2_all, up_w)
     sigma = jax.nn.sigmoid(gate)
+    act = (gate * sigma * up_val).astype(jnp.bfloat16)
+    d_act = dot_nn(d_down_all, down_w)
     d_gate = (d_act * up_val * sigma * (1.0 + gate * (1.0 - sigma))).astype(jnp.bfloat16)
     d_up = (d_act * gate * sigma).astype(jnp.bfloat16)
-    d_paired = alternate((d_gate, d_up), lanes)
-    d_n2 = fold_columns(d_paired, jnp.concatenate(slabs_back[4:6], 1))
+    d_n2_parts = dot_nt(d_gate, gate_w) + dot_nt(d_up, up_w)
+    d_n2 = scatter_tokens(
+        d_n2_parts.astype(jnp.bfloat16).reshape(lanes, token_rows, width), lanes
+    )
+    down = scatter_tokens(
+        dot_nt(act, down_w).astype(jnp.bfloat16).reshape(lanes, token_rows, width), lanes
+    )
+    mixed = (hidden + valid_col * down).astype(jnp.bfloat16)
+    grad_gate = dot_tn(normed2_all, d_gate).astype(jnp.bfloat16)
+    grad_up = dot_tn(normed2_all, d_up).astype(jnp.bfloat16)
+    grad_down = exchange(
+        dot_tn(d_down_all, act).astype(jnp.bfloat16).reshape(lanes, out_part, hidden_part), lanes
+    )
+    hidden_grads = lax.psum_scatter(
+        jnp.concatenate(
+            [
+                grad_gate.reshape(fsdp_size, rows_each, hidden_part),
+                grad_up.reshape(fsdp_size, rows_each, hidden_part),
+                grad_down.reshape(fsdp_size, rows_each, hidden_part),
+            ],
+            1,
+        ),
+        "fsdp",
+        scatter_dimension=0,
+        tiled=False,
+    ).astype(jnp.float32)
+    grad_w_gate = hidden_grads[:rows_each]
+    grad_w_up = hidden_grads[rows_each : 2 * rows_each]
+    grad_w_down = (
+        hidden_grads[2 * rows_each :]
+        .reshape(pieces_each, out_part, hidden_part)
+        .transpose(0, 2, 1)
+        .reshape(-1, out_part)
+    )
     scaled_two = d_n2 * gain_two
     dh = grad_out + inv_two * (
         scaled_two - unit_two * jnp.mean(scaled_two * unit_two, -1, keepdims=True)
     )
     grad_gain_two = jnp.sum(d_n2 * unit_two, 0)
     d_proj = (valid_col * dh).astype(jnp.bfloat16)
-    head_gradient = fold_columns(d_proj, slabs_back[3]).astype(jnp.bfloat16)
+    out_grad = lax.psum_scatter(
+        dot_tn(d_proj, heads_out).astype(jnp.bfloat16).reshape(lanes, out_part, -1),
+        "dp",
+        scatter_dimension=0,
+        tiled=False,
+    )
+    head_gradient = dot_nn(d_proj, wo_t).astype(jnp.bfloat16)
     head_gradient4 = head_gradient.reshape(token_rows, KEY_VALUE_HEADS, head_groups, HEAD_SIZE)
     delta = jnp.einsum("qgjd,qgjd->gjq", head_gradient4.astype(jnp.float32), attention_heads)
 
@@ -324,20 +414,20 @@
         jnp.zeros((token_rows, KEY_VALUE_HEADS, head_groups, HEAD_SIZE), jnp.float32),
         block_tiles,
     )
-    local_keys, own_values = (
-        lax.psum_scatter(
-            key_gradient.reshape(grouped_rows, KEY_VALUE_HEADS * HEAD_SIZE).astype(jnp.bfloat16),
-            "fsdp",
-            scatter_dimension=0,
-            tiled=True,
-        ).astype(jnp.float32),
-        lax.psum_scatter(
-            value_gradient.reshape(grouped_rows, KEY_VALUE_HEADS * HEAD_SIZE).astype(jnp.bfloat16),
-            "fsdp",
-            scatter_dimension=0,
-            tiled=True,
-        ).astype(jnp.float32),
-    )
+    own_pair = scatter_rows(
+        jnp.concatenate(
+            [
+                key_gradient.reshape(grouped_rows, KEY_VALUE_HEADS * HEAD_SIZE),
+                value_gradient.reshape(grouped_rows, KEY_VALUE_HEADS * HEAD_SIZE),
+            ],
+            1,
+        )
+        .astype(jnp.bfloat16)
+        .reshape(fsdp_size, token_rows, -1),
+        fsdp_size,
+    )
+    local_keys = own_pair[:, : KEY_VALUE_HEADS * HEAD_SIZE]
+    own_values = own_pair[:, KEY_VALUE_HEADS * HEAD_SIZE :]
     d_q_pre = (
         rotary_reverse(grad_query, cosine_table, sine_table)
         .reshape(token_rows, QUERY_HEADS * HEAD_SIZE)
@@ -351,42 +441,53 @@
         .astype(jnp.bfloat16)
     )
     d_v_pre = own_values.astype(jnp.bfloat16)
-    d_joint = alternate((d_q_pre, d_k_pre, d_v_pre), lanes)
-    d_n1 = fold_columns(d_joint, jnp.concatenate(slabs_back[0:3], 1))
+    d_joint = jnp.concatenate([d_q_pre, d_k_pre, d_v_pre], 1)
+    d_n1 = dot_nn(d_joint, joint_t)
     scaled_one = d_n1 * gain_one
     d_tokens = (
         dh + inv_one * (scaled_one - unit_one * jnp.mean(scaled_one * unit_one, -1, keepdims=True))
     ).astype(jnp.bfloat16)
     grad_gain_one = jnp.sum(d_n1 * unit_one, 0)
-    local_vectors = jnp.concatenate(
-        [
-            grad_gain_one,
-            jnp.sum(d_q_pre.astype(jnp.float32), 0),
-            jnp.sum(d_v_pre.astype(jnp.float32), 0),
-            grad_gain_two,
-        ]
-    )
-    summed_vectors = lax.psum(local_vectors, ("fsdp", "dp"))
-    dp_place = lax.axis_index("dp")
-    sections = (attn_gain.shape[0], b_query.shape[0], b_value.shape[0], mlp_gain.shape[0])
-    vector_pieces = []
-    offset = 0
-    for width in sections:
-        whole_width = width * lanes
-        vector_pieces.append(
-            lax.dynamic_slice_in_dim(summed_vectors, offset + dp_place * width, width)
-        )
-        offset = offset + whole_width
-    joint_grad, out_grad, pair_grad, down_grad = weight_grads(
-        ((normed, d_joint), (heads_out, d_proj), (normed2, d_paired), (act, d_down))
-    )
-    first_cut = joint_widths[0]
-    second_cut = joint_widths[0] + joint_widths[1]
-    grad_w_query = joint_grad[:, :first_cut]
-    grad_w_key = joint_grad[:, first_cut:second_cut]
-    grad_w_value = joint_grad[:, second_cut:]
-    grad_w_gate = pair_grad[:, : pair_widths[0]]
-    grad_w_up = pair_grad[:, pair_widths[0] :]
+    local_vectors = (
+        grad_gain_one,
+        jnp.sum(d_q_pre.astype(jnp.float32), 0),
+        jnp.sum(d_v_pre.astype(jnp.float32), 0),
+        grad_gain_two,
+    )
+    vector_rows = jnp.concatenate([v.reshape(lanes, -1) for v in local_vectors], 1)
+    vector_rows = jnp.pad(vector_rows, ((0, 0), (0, width - vector_count)))
+    vector_rows = jnp.pad(vector_rows[:, None].astype(jnp.bfloat16), ((0, 0), (0, 15), (0, 0)))
+    joint_grads = dot_tn(d_joint, normed).astype(jnp.bfloat16)
+    joint_sum = lax.psum_scatter(
+        jnp.concatenate(
+            [
+                joint_grads[:query_width].reshape(lanes, query_part, width),
+                joint_grads[query_width : query_width + key_width].reshape(lanes, key_part, width),
+                joint_grads[query_width + key_width :].reshape(lanes, key_part, width),
+                vector_rows,
+            ],
+            1,
+        ),
+        "dp",
+        scatter_dimension=0,
+        tiled=False,
+    )
+    qkv_rows = query_part + 2 * key_part
+    row_sums = scatter_rows(
+        jnp.concatenate([joint_sum[:qkv_rows], out_grad])
+        .T.reshape(fsdp_size, rows_each, joint_rows),
+        fsdp_size,
+    )
+    grad_w_query, grad_w_key, grad_w_value, out_grad = [
+        row_sums[:, edges[i] : edges[i + 1]] for i in range(4)
+    ]
+    own_vectors = joint_sum[qkv_rows, :vector_count].astype(jnp.float32)
+    vector_sum = own_vectors
+    for k in range(1, fsdp_size):
+        vector_sum = vector_sum + lax.ppermute(
+            own_vectors, "fsdp", [(i, (i + k) % fsdp_size) for i in range(fsdp_size)]
+        )
+    vector_pieces = [vector_sum[marks[i] : marks[i + 1]] for i in range(4)]
     return (
         mixed[None],
         d_tokens[None],
@@ -400,7 +501,7 @@
         vector_pieces[3],
         grad_w_gate,
         grad_w_up,
-        down_grad,
+        grad_w_down,
     )
 
 

time: 911 us -> 706 us (0.77)
  waiting for transfers between devices: 395 us -> 257 us
  blocking collectives: 144 us -> 19.5 us
  starting transfers between devices: 1.16 us -> 61.6 us
  matrix products: 203 us -> 182 us
  local copies, waits for them, and re-layouts: 81.9 us -> 95.4 us
    reduce_scatter x4 -> x3, waiting for transfers between devices: 244 us -> 83.2 us  [the longest x1 50.4 us: body(): lax.psum_scatter(jnp.concatenate([grad_gate.reshape(fsdp_size, rows_each,...]
    ppermute x0 -> x60, waiting for transfers between devices: none -> 127 us  [the longest x48 102 us: flip(): return lax.ppermute(array, 'dp', [(i, i ^ mask) for i in range(size)])]
    unnamed x23 -> x5, waiting for transfers between devices: 88.2 us -> 0.08 us
    all_gather x6 -> x1, blocking collectives: 89.5 us -> 19.5 us  [body(): lax.all_gather(jnp.concatenate([w_query, w_key, w_value, w_out], 1), 'fsd...]
    ppermute x0 -> x60, starting transfers between devices: none -> 61.1 us  [the longest x48 35.5 us: flip(): return lax.ppermute(array, 'dp', [(i, i ^ mask) for i in range(size)])]
    psum x1 -> x0, blocking collectives: 39.9 us -> none  [body(): summed_vectors = lax.psum(local_vectors, ('fsdp', 'dp'))]
    all_gather x7 -> x2, waiting for transfers between devices: 62.9 us -> 46.5 us  [the longest x1 28.4 us: body(): lax.all_gather(jnp.concatenate([projections, vector_block]), 'dp', axis=0)]
    unnamed x100 -> x148, local copies, waits for them, and re-layouts: 36.7 us -> 21.8 us
  transfers between devices with their start and end apart: 17 -> 65, of which waited for: 13 -> 32; matrix products, arithmetic and copies ran while one was open for 24% -> 24% of each run, Pallas kernels for 0% -> 0%
where the time goes in v1:
time: 706 us; the launch traced here: 698 us
  waiting for transfers between devices  257 us (36%)
  matrix products  182 us (26%)
  local copies, waits for them, and re-layouts  95.4 us (14%)
  other arithmetic  66.2 us (9%)
  starting transfers between devices  61.6 us (9%)
  blocking collectives  19.5 us (3%)
  between operations  15.5 us (2%)
    ppermute x48, waiting for transfers between devices, flip(): return lax.ppermute(array, 'dp', [(i, i ^ mask) for i in range(size)])  102 us
    reduce_scatter x1, waiting for transfers between devices, body(): lax.psum_scatter(jnp.concatenate([grad_gate.reshape(fsdp_size, rows_each,...  50.4 us
    ppermute x48, starting transfers between devices, flip(): return lax.ppermute(array, 'dp', [(i, i ^ mask) for i in range(size)])  35.5 us
    reduce_scatter x1, waiting for transfers between devices, body(): lax.psum_scatter(dot_tn(d_proj, heads_out).astype(jnp.bfloat16).reshape(l...  32.8 us
    dot_general x5, matrix products, dot_nn(): return jnp.dot(left, right, preferred_element_type=jnp.float32)  31.4 us
    dot_general x5, matrix products, dot_nt(): lax.dot_general(left, right, (((1,), (1,)), ((), ())), preferred_element_...  30.7 us
    dot_general x5, matrix products, dot_tn(): lax.dot_general(left, right, (((0,), (0,)), ((), ())), preferred_element_...  29.2 us
    all_gather x1, waiting for transfers between devices, body(): lax.all_gather(jnp.concatenate([projections, vector_block]), 'dp', axis=0)  28.4 us
  transfers between devices with their start and end apart: 65, of which 32 were waited for; matrix products, arithmetic and copies ran while one was open for 24% of the time, Pallas kernels for 0%

profile of v1, /device:TPU:0, one launch (start us, length us, event | category | flops | bytes accessed | tf_op | source)
XLA Modules:
  0.0 698.4 jit_solution(3232120959295274222)
XLA Ops:
  11.1 19.5 %all_gather.15 = bf16[896,256]{1,0:T(8,128)(2,1)S(1)} all-gather(bf16[224,256]{1,0:T(8,128)(2,1)S(1)} %pad_maximum_fusion.14), channel_id=1, replica_groups=mesh['fsdp'=4,'dp'=8] {'fsdp'}, dimensions={0}, use_global_device_ids=true | all-gather | bytes 573440 | tf_op jit(solution)/shard_map/all_gather | solution.py:216
  39.6 11.9 %collective-permute-done.28 = bf16[384,896]{1,0:T(8,128)(2,1)S(1)} collective-permute-done((bf16[384,896]{1,0:T(8,128)(2,1)}, bf16[384,896]{1,0:T(8,128)(2,1)S(1)}, u32[]{:S(2)}, u32[]{:S(2)}) %collective-permute-start.28) | collective-permute-done | bytes 688160 | tf_op jit(solution)/shard_map/ppermute | solution.py:82
  65.4 18.1 %all-gather.7.cloned.1.call-done = bf16[2688,608]{1,0:T(8,128)(2,1)} async-done(((bf16[672,608]{1,0:T(8,128)(2,1)}), bf16[2688,608]{1,0:T(8,128)(2,1)}) %all-gather.7.cloned.1.call-update) | async-done | bytes 3268624 | tf_op jit(solution)/shard_map/all_gather | solution.py:237
  93.4 28.4 %all-gather.5.cloned.1.call-done = bf16[2176,896]{1,0:T(8,128)(2,1)} async-done(((bf16[272,896]{1,0:T(8,128)(2,1)}), bf16[2176,896]{1,0:T(8,128)(2,1)}) %all-gather.5.cloned.1.call-update) | async-done | bytes 3899408 | tf_op jit(solution)/shard_map/all_gather | solution.py:223
  159.4 39.9 %while.40 = (s32[]{:T(128)}, f32[2,7,384]{2,1,0:T(8,128)S(1)}, f32[2,7,384]{2,1,0:T(8,128)S(1)}, s32[384]{0:T(512)S(1)}, s32[3,512]{1,0:T(4,128)S(1)}, /*index=5...) while((s32[]{:T(128)}, f32[2,7,384]{2,1,0:T(8,128)S(1)}, ...), condition=%wide.region_10.11_spmd.clone, body=%wide.region_7.10_spmd.clone.sunk | while | flops 375744768 | bytes 23733800 | solution.py:306
  200.7 13.6 %while.41 = (s32[]{:T(128)}, f32[384,2,7,64]{0,3,2,1:T(8,128)S(1)}, bf16[3,512,2,64]{1,3,2,0:T(8,128)(2,1)S(1)}, s32[384]{0:T(512)S(1)}, s32[3,512]{1,0:T(4,128)...) while((s32[]{:T(128)}, f32[384,2,7,64]{0,3,2,1:T(8,128)S(1)}, ...), condition=%wide.region_12.13_spmd.clone, body=%wide.region_11.12_spmd.clone.sunk | while | flops 717717504 | bytes 4146731 | solution.py:317
  228.4 8.9 %collective-permute-done.14 = bf16[1,112,608]{2,1,0:T(8,128)(2,1)S(1)} collective-permute-done((bf16[1,112,608]{2,1,0:T(8,128)(2,1)S(1)}, bf16[1,112,608]{2,1,0:T(8,128)(2,1)S(1)}, u32[]{:S(2)}, u32[]{:S(2)}) %collective-permute-start.14) | collective-permute-done | bytes 136224 | tf_op jit(solution)/shard_map/ppermute | solution.py:82
  242.3 9.0 %collective-permute-done.16 = bf16[1,112,608]{2,1,0:T(8,128)(2,1)S(1)} collective-permute-done((bf16[1,112,608]{2,1,0:T(8,128)(2,1)S(1)}, bf16[1,112,608]{2,1,0:T(8,128)(2,1)S(1)}, u32[]{:S(2)}, u32[]{:S(2)}) %collective-permute-start.16) | collective-permute-done | bytes 136224 | tf_op jit(solution)/shard_map/ppermute | solution.py:82
  261.3 7.6 %collective-permute-done.8 = bf16[192,896]{1,0:T(8,128)(2,1)S(1)} collective-permute-done((bf16[192,896]{1,0:T(8,128)(2,1)S(1)}, bf16[192,896]{1,0:T(8,128)(2,1)S(1)}, u32[]{:S(2)}, u32[]{:S(2)}) %collective-permute-start.8) | collective-permute-done | bytes 344096 | tf_op jit(solution)/shard_map/ppermute | solution.py:82
  284.3 14.7 %multiply_convert_fusion = (bf16[3072,608]{0,1:T(8,128)(2,1)S(1)}, bf16[3072,608]{0,1:T(8,128)(2,1)}, bf16[3072,608]{0,1:T(8,128)(2,1)}) fusion(f32[3072,608]{0,1:T(8,128)} %fusion.150, f32[3072,608]{0,1:T(8,128)} %fusion.151, bf16[3072,896]{1,0:T(8,128)(2,1)} %bitcast.51, bf16[896,608]{1,0:T(8,128)(2,1)} %bitcast.41), kind=kOutput, calls=%fused_computation.72 | convolution fusion | flops 3376939008 | bytes 32743424 | tf_op jit(solution)/shard_map/dot_general | solution.py:173
  299.0 11.1 %fusion.152 = f32[3072,896]{1,0:T(8,128)} fusion(bf16[3072,608]{0,1:T(8,128)(2,1)} %get-tuple-element.745, bf16[896,608]{1,0:T(8,128)(2,1)S(1)} %bitcast.416), kind=kOutput, calls=%fused_computation.320 | convolution fusion | flops 3347054592 | bytes 15835136 | tf_op jit(solution)/shard_map/dot_general | solution.py:167
  310.0 7.8 %add_convert_fusion = bf16[3072,896]{1,0:T(8,128)(2,1)S(1)} fusion(f32[3072,896]{1,0:T(8,128)} %fusion.152, bf16[3072,608]{0,1:T(8,128)(2,1)S(1)} %get-tuple-element.744, bf16[896,608]{1,0:T(8,128)(2,1)S(1)} %bitcast.414), kind=kOutput, calls=%fused_computation.71 | convolution fusion | flops 3352559616 | bytes 21340160 | tf_op jit(solution)/shard_map/dot_general | solution.py:167
  344.6 8.9 %collective-permute-done.42 = bf16[192,896]{1,0:T(8,128)(2,1)S(1)} collective-permute-done((bf16[192,896]{1,0:T(8,128)(2,1)S(1)}, bf16[192,896]{1,0:T(8,128)(2,1)S(1)}, u32[]{:S(2)}, u32[]{:S(2)}) %collective-permute-start.42) | collective-permute-done | bytes 344096 | tf_op jit(solution)/shard_map/ppermute | solution.py:82
  360.5 11.7 %collective-permute-done.40 = bf16[384,896]{1,0:T(8,128)(2,1)} collective-permute-done((bf16[384,896]{1,0:T(8,128)(2,1)}, bf16[384,896]{1,0:T(8,128)(2,1)}, u32[]{:S(2)}, u32[]{:S(2)}) %collective-permute-start.40) | collective-permute-done | bytes 688160 | tf_op jit(solution)/shard_map/ppermute | solution.py:82
  376.8 8.2 %collective-permute-done.23 = bf16[384,896]{1,0:T(8,128)(2,1)} collective-permute-done((bf16[384,896]{1,0:T(8,128)(2,1)}, bf16[384,896]{1,0:T(8,128)(2,1)}, u32[]{:S(2)}, u32[]{:S(2)}) %collective-permute-start.23) | collective-permute-done | bytes 688160 | tf_op jit(solution)/shard_map/ppermute | solution.py:82
  397.0 80.3 %while.42 = (s32[]{:T(128)}, f32[384,2,7,64]{0,3,2,1:T(8,128)S(1)}, bf16[3,512,2,64]{1,3,2,0:T(8,128)(2,1)}, bf16[3,512,2,64]{1,3,2,0:T(8,128)(2,1)}, bf16[3,512...) while((s32[]{:T(128)}, f32[384,2,7,64]{0,3,2,1:T(8,128)S(1)}, ...), condition=%wide.region_16.17_spmd.clone, body=%wide.region_15.16_spmd.clone.sunk | while | flops 1791606784 | bytes 126026496 | solution.py:412
  416.6 7.4 %fusion.228 = bf16[3,512,2,64]{1,3,2,0:T(8,128)(2,1)} fusion(bf16[3,512,2,64]{1,3,2,0:T(8,128)(2,1)} %get-tuple-element.1234, s32[]{:T(128)} %get-tuple-element.1231, bf16[384,2,7,64]{0,3,2,1:T(8,128)(2,1)S(1)} %get-tuple-element.1267, f32[2,512,384,7]{2,1,3,0:T(8,128)} %copy-done.1, f32[2,7,384]{2,1,0:T(8,128)S(1)} %copy-done.54, ...), kind=kOutput, calls=%fused_computation.49.clone.1 | convolution fusion | flops 363331584 | bytes 12178944 | tf_op jit(solution)/shard_map/while/body/eval_jaxpr/gjqk,qgjd->kgd/dot_general | solution.py:389
  516.1 8.7 %convolution_convert_fusion.3 = bf16[896,608]{0,1:T(8,128)(2,1)} fusion(bf16[3072,608]{0,1:T(8,128)(2,1)} %get-tuple-element.746, bf16[3072,896]{1,0:T(8,128)(2,1)} %bitcast.51), kind=kOutput, calls=%fused_computation.95 | convolution fusion | flops 3347599360 | bytes 10330112 | tf_op jit(solution)/shard_map/dot_general | solution.py:161
  529.7 9.2 %convolution_convert_fusion.5 = bf16[896,608]{0,1:T(8,128)(2,1)} fusion(bf16[3072,608]{0,1:T(8,128)(2,1)} %get-tuple-element.745, bf16[3072,896]{1,0:T(8,128)(2,1)} %bitcast.446), kind=kOutput, calls=%fused_computation.97 | convolution fusion | flops 3347599360 | bytes 10330112 | tf_op jit(solution)/shard_map/dot_general | solution.py:161
  540.9 7.6 %convolution_convert_fusion.4 = bf16[896,608]{0,1:T(8,128)(2,1)} fusion(bf16[3072,608]{0,1:T(8,128)(2,1)S(1)} %copy-done.68, bf16[3072,896]{1,0:T(8,128)(2,1)} %bitcast.447), kind=kOutput, calls=%fused_computation.96 | convolution fusion | flops 3347599360 | bytes 10330112 | tf_op jit(solution)/shard_map/dot_general | solution.py:161
  558.6 7.9 %collective-permute-done.56 = bf16[1,112,608]{2,1,0:T(8,128)(2,1)S(1)} collective-permute-done((bf16[1,112,608]{2,1,0:T(8,128)(2,1)S(1)}, bf16[1,112,608]{2,1,0:T(8,128)(2,1)S(1)}, u32[]{:S(2)}, u32[]{:S(2)}) %collective-permute-start.56) | collective-permute-done | bytes 136224 | tf_op jit(solution)/shard_map/ppermute | solution.py:82
  585.0 32.8 %reduce-scatter.6.cloned.1.call-done = bf16[1,112,896]{2,1,0:T(8,128)(2,1)} async-done(((bf16[8,112,896]{2,1,0:T(8,128)(2,1)}), bf16[1,112,896]{2,1,0:T(8,128)(2,1)}) %reduce-scatter.6.cloned.1.call-update) | async-done | bytes 200720 | tf_op jit(solution)/shard_map/reduce_scatter | solution.py:376
  627.0 7.6 %collective-permute-done.51 = bf16[224,256]{1,0:T(8,128)(2,1)S(1)} collective-permute-done((bf16[224,256]{1,0:T(8,128)(2,1)S(1)}, bf16[224,256]{1,0:T(8,128)(2,1)S(1)}, u32[]{:S(2)}, u32[]{:S(2)}) %collective-permute-start.51) | collective-permute-done | bytes 114720 | tf_op jit(solution)/shard_map/ppermute | solution.py:154
  636.8 50.4 %reduce-scatter.8.cloned.1.call-done = bf16[1,672,608]{2,1,0:T(8,128)(2,1)} async-done(((bf16[4,672,608]{2,1,0:T(8,128)(2,1)}), bf16[1,672,608]{2,1,0:T(8,128)(2,1)}) %reduce-scatter.8.cloned.1.call-update) | async-done | bytes 817168 | tf_op jit(solution)/shard_map/reduce_scatter | solution.py:349
  (552 shorter events, 384.3 us)
Async XLA Ops:
  7.2 76.4 %all-gather.7.cloned.1.call-start = ((), (), s32[]{:S(2)}) async-start(), calls=%async_computation.7 | async-start | bytes 4300800 | tf_op jit(solution)/shard_map/all_gather | solution.py:237
  10.7 111.1 %all-gather.5.cloned.1.call-start = ((), (), s32[]{:S(2)}) async-start(), calls=%async_computation.6 | async-start | bytes 4386816 | tf_op jit(solution)/shard_map/all_gather | solution.py:223
  31.9 544.5 %reduce-scatter.4.cloned.1.call-start = ((), (), s32[]{:S(2)}) async-start(), calls=%async_computation.3 | async-start | bytes 2580480 | tf_op jit(solution)/shard_map/reduce_scatter | solution.py:461
  33.4 21.4 %collective-permute-start.27 = (bf16[384,896]{1,0:T(8,128)(2,1)}, bf16[384,896]{1,0:T(8,128)(2,1)}, u32[]{:S(2)}, u32[]{:S(2)}) collective-permute-start(bf16[384,896]{1,0:T(8,128)(2,1)} %fusion.69), channel_id=1, source_target_pairs={{0,1},{1,0},{2,3},{3,2},{4,5},{5,4},{6,7},{7,6},{8,9},{9,8},{10,11... | collective-permute-start | bytes 2064392 | tf_op jit(solution)/shard_map/ppermute | solution.py:82
  54.8 33.7 %collective-permute-start.31 = (bf16[384,896]{1,0:T(8,128)(2,1)S(1)}, bf16[384,896]{1,0:T(8,128)(2,1)S(1)}, u32[]{:S(2)}, u32[]{:S(2)}) collective-permute-start(bf16[384,896]{1,0:T(8,128)(2,1)S(1)} %collective-permute-done.30), channel_id=1, source_target_pairs={{0,1},{1,0},{2,3},{3,2},{4,5},{5,4},{6,7},{7,6},{8,9},{9,8},{10,11... | collective-permute-start | bytes 2064392 | tf_op jit(solution)/shard_map/ppermute | solution.py:82
  62.2 160.2 %collective-permute-start.34 = (bf16[192,896]{1,0:T(8,128)(2,1)}, bf16[192,896]{1,0:T(8,128)(2,1)}, u32[]{:S(2)}, u32[]{:S(2)}) collective-permute-start(bf16[192,896]{1,0:T(8,128)(2,1)} %collective-permute-done.32), channel_id=1, source_target_pairs={{0,1},{1,0},{2,3},{3,2},{4,5},{5,4},{6,7},{7,6},{8,9},{9,8},{10,11... | collective-permute-start | bytes 1032200 | tf_op jit(solution)/shard_map/ppermute | solution.py:82
  63.5 158.8 %collective-permute-start.35 = (bf16[192,896]{1,0:T(8,128)(2,1)}, bf16[192,896]{1,0:T(8,128)(2,1)}, u32[]{:S(2)}, u32[]{:S(2)}) collective-permute-start(bf16[192,896]{1,0:T(8,128)(2,1)} %collective-permute-done.33), channel_id=1, source_target_pairs={{0,1},{1,0},{2,3},{3,2},{4,5},{5,4},{6,7},{7,6},{8,9},{9,8},{10,11... | collective-permute-start | bytes 1032200 | tf_op jit(solution)/shard_map/ppermute | solution.py:82
  91.9 134.2 %collective-permute-start.13 = (bf16[1,112,608]{2,1,0:T(8,128)(2,1)}, bf16[1,112,608]{2,1,0:T(8,128)(2,1)}, u32[]{:S(2)}, u32[]{:S(2)}) collective-permute-start(bf16[1,112,608]{2,1,0:T(8,128)(2,1)} %get-tuple-element.792), channel_id=1, source_target_pairs={{0,2},{1,3},{2,0},{3,1},{4,6},{5,7},{6,4},{7,5},{8,10},{9,11},{10,... | collective-permute-start | bytes 408584 | tf_op jit(solution)/shard_map/ppermute | solution.py:82
  218.9 34.5 %collective-permute-start.4 = (bf16[384,896]{1,0:T(8,128)(2,1)S(1)}, bf16[384,896]{1,0:T(8,128)(2,1)S(1)}, u32[]{:S(2)}, u32[]{:S(2)}) collective-permute-start(bf16[384,896]{1,0:T(8,128)(2,1)S(1)} %get-tuple-element.729), channel_id=1, source_target_pairs={{0,2},{1,3},{2,0},{3,1},{4,6},{5,7},{6,4},{7,5},{8,10},{9,11},{10,... | collective-permute-start | bytes 2064392 | tf_op jit(solution)/shard_map/ppermute | solution.py:82
  225.0 36.1 %collective-permute-start.3 = (bf16[384,896]{1,0:T(8,128)(2,1)S(1)}, bf16[384,896]{1,0:T(8,128)(2,1)S(1)}, u32[]{:S(2)}, u32[]{:S(2)}) collective-permute-start(bf16[384,896]{1,0:T(8,128)(2,1)S(1)} %get-tuple-element.729), channel_id=1, source_target_pairs={{0,1},{1,0},{2,3},{3,2},{4,5},{5,4},{6,7},{7,6},{8,9},{9,8},{10,11... | collective-permute-start | bytes 2064392 | tf_op jit(solution)/shard_map/ppermute | solution.py:82
  226.1 34.1 %collective-permute-start.6 = (bf16[384,896]{1,0:T(8,128)(2,1)S(1)}, bf16[384,896]{1,0:T(8,128)(2,1)S(1)}, u32[]{:S(2)}, u32[]{:S(2)}) collective-permute-start(bf16[384,896]{1,0:T(8,128)(2,1)S(1)} %get-tuple-element.729), channel_id=1, source_target_pairs={{0,4},{1,5},{2,6},{3,7},{4,0},{5,1},{6,2},{7,3},{8,12},{9,13},{10,... | collective-permute-start | bytes 2064392 | tf_op jit(solution)/shard_map/ppermute | solution.py:82
  330.6 46.2 %collective-permute-start.19 = (bf16[384,896]{1,0:T(8,128)(2,1)}, bf16[384,896]{1,0:T(8,128)(2,1)}, u32[]{:S(2)}, u32[]{:S(2)}) collective-permute-start(bf16[384,896]{1,0:T(8,128)(2,1)} %get-tuple-element.754), channel_id=1, source_target_pairs={{0,1},{1,0},{2,3},{3,2},{4,5},{5,4},{6,7},{7,6},{8,9},{9,8},{10,11... | collective-permute-start | bytes 2064392 | tf_op jit(solution)/shard_map/ppermute | solution.py:82
  330.8 29.1 %collective-permute-start.36 = (bf16[384,896]{1,0:T(8,128)(2,1)S(1)}, bf16[384,896]{1,0:T(8,128)(2,1)S(1)}, u32[]{:S(2)}, u32[]{:S(2)}) collective-permute-start(bf16[384,896]{1,0:T(8,128)(2,1)S(1)} %get-tuple-element.747), channel_id=1, source_target_pairs={{0,1},{1,0},{2,3},{3,2},{4,5},{5,4},{6,7},{7,6},{8,9},{9,8},{10,11... | collective-permute-start | bytes 2064392 | tf_op jit(solution)/shard_map/ppermute | solution.py:82
  335.3 20.1 %collective-permute-start.22 = (bf16[192,896]{1,0:T(8,128)(2,1)S(1)}, bf16[192,896]{1,0:T(8,128)(2,1)S(1)}, u32[]{:S(2)}, u32[]{:S(2)}) collective-permute-start(bf16[192,896]{1,0:T(8,128)(2,1)S(1)} %get-tuple-element.801), channel_id=1, source_target_pairs={{0,4},{1,5},{2,6},{3,7},{4,0},{5,1},{6,2},{7,3},{8,12},{9,13},{10,... | collective-permute-start | bytes 1032200 | tf_op jit(solution)/shard_map/ppermute | solution.py:82
  336.1 21.5 %collective-permute-start.25 = (bf16[192,896]{1,0:T(8,128)(2,1)S(1)}, bf16[192,896]{1,0:T(8,128)(2,1)S(1)}, u32[]{:S(2)}, u32[]{:S(2)}) collective-permute-start(bf16[192,896]{1,0:T(8,128)(2,1)S(1)} %get-tuple-element.802), channel_id=1, source_target_pairs={{0,2},{1,3},{2,0},{3,1},{4,6},{5,7},{6,4},{7,5},{8,10},{9,11},{10,... | collective-permute-start | bytes 1032200 | tf_op jit(solution)/shard_map/ppermute | solution.py:82
  353.5 18.7 %collective-permute-start.40 = (bf16[384,896]{1,0:T(8,128)(2,1)}, bf16[384,896]{1,0:T(8,128)(2,1)}, u32[]{:S(2)}, u32[]{:S(2)}) collective-permute-start(bf16[384,896]{1,0:T(8,128)(2,1)} %pad_maximum_fusion.8), channel_id=1, source_target_pairs={{0,2},{1,3},{2,0},{3,1},{4,6},{5,7},{6,4},{7,5},{8,10},{9,11},{10,... | collective-permute-start | bytes 2064392 | tf_op jit(solution)/shard_map/ppermute | solution.py:82
  355.5 18.7 %collective-permute-start.43 = (bf16[384,896]{1,0:T(8,128)(2,1)}, bf16[384,896]{1,0:T(8,128)(2,1)}, u32[]{:S(2)}, u32[]{:S(2)}) collective-permute-start(bf16[384,896]{1,0:T(8,128)(2,1)} %pad_maximum_fusion.9), channel_id=1, source_target_pairs={{0,4},{1,5},{2,6},{3,7},{4,0},{5,1},{6,2},{7,3},{8,12},{9,13},{10,... | collective-permute-start | bytes 2064392 | tf_op jit(solution)/shard_map/ppermute | solution.py:82
  357.7 27.4 %collective-permute-start.23 = (bf16[384,896]{1,0:T(8,128)(2,1)}, bf16[384,896]{1,0:T(8,128)(2,1)}, u32[]{:S(2)}, u32[]{:S(2)}) collective-permute-start(bf16[384,896]{1,0:T(8,128)(2,1)} %pad_maximum_fusion.6), channel_id=1, source_target_pairs={{0,2},{1,3},{2,0},{3,1},{4,6},{5,7},{6,4},{7,5},{8,10},{9,11},{10,... | collective-permute-start | bytes 2064392 | tf_op jit(solution)/shard_map/ppermute | solution.py:82
  359.9 26.9 %collective-permute-start.26 = (bf16[384,896]{1,0:T(8,128)(2,1)}, bf16[384,896]{1,0:T(8,128)(2,1)}, u32[]{:S(2)}, u32[]{:S(2)}) collective-permute-start(bf16[384,896]{1,0:T(8,128)(2,1)} %pad_maximum_fusion.7), channel_id=1, source_target_pairs={{0,4},{1,5},{2,6},{3,7},{4,0},{5,1},{6,2},{7,3},{8,12},{9,13},{10,... | collective-permute-start | bytes 2064392 | tf_op jit(solution)/shard_map/ppermute | solution.py:82
  516.0 101.7 %reduce-scatter.6.cloned.1.call-start = ((), (), s32[]{:S(2)}) async-start(), calls=%async_computation.4 | async-start | bytes 1806336 | tf_op jit(solution)/shard_map/reduce_scatter | solution.py:376
  529.4 157.8 %reduce-scatter.8.cloned.1.call-start = ((), (), s32[]{:S(2)}) async-start(), calls=%async_computation.5 | async-start | bytes 4300800 | tf_op jit(solution)/shard_map/reduce_scatter | solution.py:349
  577.1 45.8 %collective-permute-start.47 = (f32[352]{0:T(512)S(1)}, f32[352]{0:T(512)S(1)}, u32[]{:S(2)}, u32[]{:S(2)}) collective-permute-start(f32[352]{0:T(512)S(1)} %fusion.125), channel_id=1, source_target_pairs={{0,8},{8,16},{16,24},{24,0},{1,9},{9,17},{17,25},{25,1},{2,10},{10... | collective-permute-start | bytes 4232 | tf_op jit(solution)/shard_map/ppermute | solution.py:487
  581.5 42.8 %collective-permute-start.48 = (f32[352]{0:T(512)S(1)}, f32[352]{0:T(512)S(1)}, u32[]{:S(2)}, u32[]{:S(2)}) collective-permute-start(f32[352]{0:T(512)S(1)} %fusion.125), channel_id=1, source_target_pairs={{0,16},{8,24},{16,0},{24,8},{1,17},{9,25},{17,1},{25,9},{2,18},{10... | collective-permute-start | bytes 4232 | tf_op jit(solution)/shard_map/ppermute | solution.py:487
  583.7 40.6 %collective-permute-start.49 = (f32[352]{0:T(512)S(1)}, f32[352]{0:T(512)S(1)}, u32[]{:S(2)}, u32[]{:S(2)}) collective-permute-start(f32[352]{0:T(512)S(1)} %fusion.125), channel_id=1, source_target_pairs={{0,24},{8,0},{16,8},{24,16},{1,25},{9,1},{17,9},{25,17},{2,26},{10... | collective-permute-start | bytes 4232 | tf_op jit(solution)/shard_map/ppermute | solution.py:487
  (123 other events, 1276.0 us)
Sparse Core Ops, SparseCore 0:
  10.8 72.6 all-gather.6
  86.0 35.7 all-gather.4
  516.1 56.0 reduce-scatter.3
  575.9 41.8 reduce-scatter.5
  619.9 67.2 reduce-scatter.7
